TPU v7x, 512 devices: a whole 4x8x8 slice. The times are simulated.
512 devices in a mesh: grp: 16 (over z, core), aux: 32 (over x, y).
Axes of the slice: x: 4, y: 8, z: 8, core: 2. Of those that a mesh axis runs over, the one named last changes fastest.
Arguments:
- integrals: bfloat16 [2048, 262144], P('aux', 'grp'), parts along dimension 1, may hold values from -6 to 6
- inverses: bfloat16 [4, 512, 512], P(None, 'aux'), as said below
- lower_blocks: bfloat16 [6, 512, 512], P(None, 'aux'), may hold values from -0.25 to 0.25
Outputs:
- solved: bfloat16 [2048, 262144], P(None, ('grp', 'aux')), parts along dimension 1
There are 16 independent parts, one for each index of `grp`. A program takes and returns all parts, laid end to end along the dimension named above; an argument that names none is the same for every part. Nothing has to cross between parts.
Inputs may be any that keep to these rules, and one draw needn't show every extreme that they name: Each inverses[k] is lower triangular with diagonal entries between 0.5 and 1.5.
All inputs are finite; a program needn't handle non-finite values.
Results may differ from a plain program's by a relative error of at most 0.007.
Values may be sent and summed in bfloat16 or wider, within the bound.
No kernel may reach another device: no remote copies, remote signals or barrier semaphores. Data moves between devices by JAX's collectives and lax.ppermute only.
A program may use at most 64 MiB of HBM per device.

v0:
```python
import jax
import jax.numpy as jnp
from jax import lax
from jax.sharding import PartitionSpec as P


def local(integrals, inverses, lower_blocks):
    inv_all, low_all = (
        lax.all_gather(inverses, "aux", axis=1, tiled=True),
        lax.all_gather(lower_blocks, "aux", axis=1, tiled=True),
    )
    count = inv_all.shape[0]
    panel = inv_all.shape[1]
    width = integrals.shape[0]
    groups = lax.axis_size("aux")
    rows = integrals.shape[1] // groups
    sectioned = integrals.reshape(width, groups, rows)
    block = lax.all_to_all(sectioned, "aux", split_axis=1, concat_axis=0, tiled=True)
    columns = block.reshape(block.shape[0], block.shape[2])
    outs = []
    for k in range(count):
        acc = columns[k * panel : (k + 1) * panel].astype(jnp.float32)
        for j in range(k):
            acc = acc - jnp.dot(
                low_all[k * (k - 1) // 2 + j], outs[j], preferred_element_type=jnp.float32
            )
        rest = acc.astype(jnp.bfloat16)
        outs.append(
            jnp.dot(inv_all[k], rest, preferred_element_type=jnp.float32).astype(jnp.bfloat16)
        )
    return jnp.concatenate(outs, axis=0)


def solution(mesh):
    placed = (P("aux", "grp"), P(None, "aux", None), P(None, "aux", None))
    return jax.shard_map(
        local, mesh=mesh, in_specs=placed, out_specs=P(None, ("grp", "aux")), check_vma=False
    )
```

profile of v0, /device:TPU:64, one launch (start us, length us, event | category | flops | bytes accessed | tf_op | source)
XLA Modules:
  0.0 209.6 jit_solution(11446586706947685064)
XLA Ops:
  6.5 0.0 all-gather.3.cloned.1.call-start
  6.5 0.7 all-gather.3.cloned.1.call-update
  7.3 0.0 all-gather.5.cloned.1.call-start
  7.3 0.7 all-gather.5.cloned.1.call-update
  8.0 1.9 copy.17
  9.9 63.3 %all_to_all.15 = bf16[64,32,512]{2,0,1:T(8,128)(2,1)S(1)} all-to-all(bf16[64,32,512]{2,0,1:T(8,128)(2,1)S(1)} %bitcast.100), channel_id=1, replica_groups=mesh['grp'=16,'aux'=32] {'aux'}, dimensions={1} | all-to-all | bytes 4194304 | tf_op jit(solution)/shard_map/all_to_all | solution.py:18
  73.2 0.1 fusion.10
  73.3 0.2 bitcast_convert_fusion.2
  73.5 1.4 copy.12
  74.8 1.3 bitcast_convert_fusion
  76.2 0.3 copy.13
  76.5 1.6 copy.14
  78.1 24.0 %all-gather.3.cloned.1.call-done = bf16[4,512,512]{2,1,0:T(8,128)(2,1)} async-done(((bf16[4,16,512]{2,1,0:T(8,128)(2,1)}), bf16[4,512,512]{2,1,0:T(8,128)(2,1)}) %all-gather.3.cloned.1.call-update) | async-done | bytes 2097168 | tf_op jit(solution)/shard_map/all_gather | solution.py:9
  102.1 1.5 convolution_convert_fusion.3
  103.6 84.3 %all-gather.5.cloned.1.call-done = bf16[6,512,512]{2,1,0:T(8,128)(2,1)} async-done(((bf16[6,16,512]{2,1,0:T(8,128)(2,1)}), bf16[6,512,512]{2,1,0:T(8,128)(2,1)}) %all-gather.5.cloned.1.call-update) | async-done | bytes 3145744 | tf_op jit(solution)/shard_map/all_gather | solution.py:10
  187.9 2.4 %convolution_convert_fusion.2 = bf16[512,512]{0,1:T(8,128)(2,1)S(1)} fusion(f32[512,512]{0,1:T(8,128)} %copy.12, bf16[512,512]{1,0:T(8,128)(2,1)S(1)} %convolution_convert_fusion.3, bf16[4,512,512]{2,1,0:T(8,128)(2,1)} %all-gather.3.cloned.1.call-done, bf16[6,512,512]{2,1,0:T(8,128)(2,1)} %all-gather.5.cloned.1.call-done), kind=kOutput, calls=%fused_computation.16 | convolution fusion | flops 537657344 | bytes 3145728 | tf_op jit(solution)/shard_map/dot_general | solution.py:29
  190.3 2.5 %fusion.4 = f32[512,512]{0,1:T(8,128)} fusion(f32[512,512]{0,1:T(8,128)S(1)} %copy.13, bf16[512,512]{1,0:T(8,128)(2,1)S(1)} %convolution_convert_fusion.3, bf16[6,512,512]{2,1,0:T(8,128)(2,1)} %all-gather.5.cloned.1.call-done), kind=kOutput, calls=%fused_computation.11 | convolution fusion | flops 268697600 | bytes 3145728 | tf_op jit(solution)/shard_map/dot_general | solution.py:24
  192.8 1.5 fusion.2
  194.3 3.2 %convolution_convert_fusion.1 = bf16[512,512]{0,1:T(8,128)(2,1)} fusion(f32[512,512]{0,1:T(8,128)} %fusion.4, bf16[512,512]{0,1:T(8,128)(2,1)S(1)} %convolution_convert_fusion.2, bf16[4,512,512]{2,1,0:T(8,128)(2,1)} %all-gather.3.cloned.1.call-done, bf16[6,512,512]{2,1,0:T(8,128)(2,1)} %all-gather.5.cloned.1.call-done), kind=kOutput, calls=%fused_computation.15 | convolution fusion | flops 537657344 | bytes 3145728 | tf_op jit(solution)/shard_map/dot_general | solution.py:29
  197.5 1.5 fusion.1
  199.0 0.0 copy-start
  199.0 2.3 %fusion.9 = bf16[512,512]{1,0:T(8,128)(2,1)S(1)} fusion(f32[512,512]{0,1:T(8,128)S(1)} %fusion.1, bf16[512,512]{0,1:T(8,128)(2,1)} %convolution_convert_fusion.1, bf16[4,512,512]{2,1,0:T(8,128)(2,1)} %all-gather.3.cloned.1.call-done, bf16[6,512,512]{2,1,0:T(8,128)(2,1)} %all-gather.5.cloned.1.call-done), kind=kOutput, calls=%fused_computation.21 | convolution fusion | flops 537657344 | bytes 3145728 | tf_op jit(solution)/shard_map/dot_general | solution.py:29
  201.3 0.0 copy-done
  201.3 1.5 pad_maximum_fusion
Async XLA Ops:
  6.5 95.6 %all-gather.3.cloned.1.call-start = ((), (), s32[]{:S(2)}) async-start(), calls=%async_computation.1 | async-start | bytes 2162688 | tf_op jit(solution)/shard_map/all_gather | solution.py:9
  7.3 180.6 %all-gather.5.cloned.1.call-start = ((), (), s32[]{:S(2)}) async-start(), calls=%async_computation.2 | async-start | bytes 3244032 | tf_op jit(solution)/shard_map/all_gather | solution.py:10
  199.0 2.3 %copy-start = (bf16[512,512]{0,1:T(8,128)(2,1)S(1)}, bf16[512,512]{0,1:T(8,128)(2,1)}, u32[]{:S(2)}) copy-start(bf16[512,512]{0,1:T(8,128)(2,1)} %convolution_convert_fusion.1) | copy-start | bytes 1572868
Sparse Core Ops, SparseCore 0:
  10.5 91.5 all-gather.2
  105.3 82.5 all-gather.4
where the time goes:
time: 210 us
  waiting for transfers between devices  110 us (52%)
  blocking collectives  63.3 us (30%)
  matrix products  14.8 us (7%)
  between operations  13.5 us (6%)
  local copies, waits for them, and re-layouts  5.24 us (2%)
  other arithmetic  2.94 us (1%)
    all_gather x1, waiting for transfers between devices, local(): lax.all_gather(lower_blocks, 'aux', axis=1, tiled=True)  84.3 us
    all_to_all x1, blocking collectives, local(): lax.all_to_all(sectioned, 'aux', split_axis=1, concat_axis=0, tiled=True)  63.3 us
    all_gather x1, waiting for transfers between devices, local(): lax.all_gather(inverses, 'aux', axis=1, tiled=True)  24 us
    dot_general x4, matrix products, local(): jnp.dot(inv_all[k], rest, preferred_element_type=jnp.float32)  9.29 us
    dot_general x3, matrix products, local(): jnp.dot(low_all[k * (k - 1) // 2 + j], outs[j], preferred_element_type=jn...  5.55 us
  transfers between devices with their start and end apart: 2, of which 2 were waited for; matrix products, arithmetic and copies ran while one was open for 4% of the time, Pallas kernels for 0%

commit v1 on v0

--- a/solution.py
+++ b/solution.py
@@ -6,7 +6,9 @@
 
 def local(integrals, inverses, lower_blocks):
     inv_all, low_all = (
-        lax.all_gather(inverses, "aux", axis=1, tiled=True),
+        jnp.concatenate(
+            lax.all_to_all(jnp.stack([inverses] * lax.axis_size("aux")), "aux", 0, 0), axis=1
+        ),
         lax.all_gather(lower_blocks, "aux", axis=1, tiled=True),
     )
     count = inv_all.shape[0]

time: 210 us -> 173 us (0.82)
  the two profiles are of different devices: /device:TPU:64 before, /device:TPU:256 now
where the time goes in v1:
time: 173 us; the launch traced here: 172 us
  waiting for transfers between devices  109 us (63%)
  starting transfers between devices  15.4 us (9%)
  matrix products  15 us (9%)
  local copies, waits for them, and re-layouts  14.7 us (8%)
  between operations  13.5 us (8%)
  other arithmetic  4.41 us (3%)
    all_to_all x1, waiting for transfers between devices, local(): lax.all_to_all(jnp.stack([inverses] * lax.axis_size('aux')), 'aux', 0, 0)  54.9 us
    all_to_all x1, waiting for transfers between devices, local(): lax.all_to_all(sectioned, 'aux', split_axis=1, concat_axis=0, tiled=True)  53.8 us
    all_to_all x1, starting transfers between devices, local(): lax.all_to_all(sectioned, 'aux', split_axis=1, concat_axis=0, tiled=True)  10.1 us
    dot_general x4, matrix products, local(): jnp.dot(inv_all[k], rest, preferred_element_type=jnp.float32)  8.08 us
    dot_general x3, matrix products, local(): jnp.dot(low_all[k * (k - 1) // 2 + j], outs[j], preferred_element_type=jn...  6.91 us
    convert_element_type x3, local copies, waits for them, and re-layouts, local(): acc = columns[k * panel:(k + 1) * panel].astype(jnp.float32)  5.43 us
    all_to_all x1, starting transfers between devices, local(): lax.all_to_all(jnp.stack([inverses] * lax.axis_size('aux')), 'aux', 0, 0)  5.29 us
  transfers between devices with their start and end apart: 3, of which 2 were waited for; matrix products, arithmetic and copies ran while one was open for 8% of the time, Pallas kernels for 0%

profile of v1, /device:TPU:256, one launch (start us, length us, event | category | flops | bytes accessed | tf_op | source)
XLA Modules:
  0.0 172.4 jit_solution(17540865308857866971)
XLA Ops:
  6.5 3.2 %copy.17 = bf16[8,32,8,512]{3,2,0,1:T(8,128)(2,1)} copy(bf16[8,32,8,512]{3,2,1,0:T(8,128)(2,1)} %bitcast.99) | data formatting | bytes 4194304 | tf_op jit(solution)/shard_map/reshape | solution.py:19
  9.7 10.1 %all-to-all-start.1 = ((bf16[64,32,512]{2,0,1:T(8,128)(2,1)}), bf16[64,32,512]{2,0,1:T(8,128)(2,1)S(1)}, u32[]{:S(2)}, u32[]{:S(2)}) async-start(bf16[64,32,512]{2,0,1:T(8,128)(2,1)} %bitcast.98), calls=%async_computation.1 | async-start | bytes 4194304 | tf_op jit(solution)/shard_map/all_to_all | solution.py:20
  19.9 0.7 all-gather.2.cloned.1.call-update
  20.6 53.8 %all-to-all-done.1 = bf16[64,32,512]{2,0,1:T(8,128)(2,1)S(1)} async-done(((bf16[64,32,512]{2,0,1:T(8,128)(2,1)}), bf16[64,32,512]{2,0,1:T(8,128)(2,1)S(1)}, u32[]{:S(2)}, u32[]{:S(2)}) %all-to-all-start.1) | async-done | bytes 2097184 | tf_op jit(solution)/shard_map/all_to_all | solution.py:20
  74.4 1.8 %stack.2 = bf16[32,4,16,512]{3,2,1,0:T(8,128)(2,1)} broadcast(bf16[4,16,512]{2,1,0:T(8,128)(2,1)S(1)} %copy-done.5), dimensions={1,2,3} | broadcast | bytes 2162688 | tf_op jit(solution)/shard_map/stack | solution.py:10
  76.2 0.3 copy-done
  76.4 5.3 %all-to-all-start = ((bf16[32,4,16,512]{3,2,1,0:T(8,128)(2,1)}), bf16[32,4,16,512]{3,2,1,0:T(8,128)(2,1)S(1)}, u32[]{:S(2)}, u32[]{:S(2)}) async-start(bf16[32,4,16,512]{3,2,1,0:T(8,128)(2,1)} %stack.2), calls=%async_computation | async-start | bytes 4194304 | tf_op jit(solution)/shard_map/all_to_all | solution.py:10
  81.7 2.7 %fusion.10 = (bf16[8,64,1,512]{3,1,0,2:T(8,128)(2,1)}, bf16[8,64,1,512]{3,1,0,2:T(8,128)(2,1)}, bf16[8,64,1,512]{3,1,0,2:T(8,128)(2,1)S(1)}, bf16[8,64,1,512]{3,1,0,2:T(8,128)(2,1)}) fusion(bf16[32,64,1,512]{3,1,0,2:T(8,128)(2,1)} %bitcast.97), kind=kLoop, calls=%fused_computation.31 | loop fusion | bytes 4194304 | tf_op jit(solution)/shard_map/slice | solution.py:24
  84.4 0.2 bitcast_convert_fusion.2
  84.6 1.3 copy.12
  85.9 2.8 %bitcast_convert_fusion = (f32[512,512]{1,0:T(8,128)}, f32[512,512]{1,0:T(8,128)}) fusion(bf16[8,64,1,512]{3,1,0,2:T(8,128)(2,1)} %get-tuple-element.6, bf16[8,64,1,512]{3,1,0,2:T(8,128)(2,1)} %get-tuple-element.5), kind=kLoop, calls=%fused_computation.28 | loop fusion | flops 524288 | bytes 3145728 | tf_op jit(solution)/shard_map/convert_element_type | solution.py:24
  88.7 1.6 copy.13
  90.3 2.5 %copy.14 = f32[512,512]{0,1:T(8,128)} copy(f32[512,512]{1,0:T(8,128)} %get-tuple-element.13) | data formatting | bytes 2097152 | tf_op jit(solution)/shard_map/convert_element_type | solution.py:24
  92.8 54.9 %all-to-all-done = bf16[32,4,16,512]{3,2,1,0:T(8,128)(2,1)S(1)} async-done(((bf16[32,4,16,512]{3,2,1,0:T(8,128)(2,1)}), bf16[32,4,16,512]{3,2,1,0:T(8,128)(2,1)S(1)}, u32[]{:S(2)}, u32[]{:S(2)}) %all-to-all-start) | async-done | bytes 2097184 | tf_op jit(solution)/shard_map/all_to_all | solution.py:10
  147.8 1.2 fusion.11
  149.0 0.1 copy-done.1
  149.1 0.4 convolution_convert_fusion.3
  149.5 2.5 %fusion.4 = f32[512,512]{0,1:T(8,128)} fusion(f32[512,512]{0,1:T(8,128)S(1)} %copy.13, bf16[512,512]{1,0:T(8,128)(2,1)S(1)} %convolution_convert_fusion.3, bf16[6,512,512]{2,1,0:T(8,128)(2,1)} %all-gather.2.cloned.1.call-done), kind=kOutput, calls=%fused_computation.11 | convolution fusion | flops 268697600 | bytes 3145728 | tf_op jit(solution)/shard_map/dot_general | solution.py:26
  152.1 1.9 %fusion.2 = f32[512,512]{0,1:T(8,128)S(1)} fusion(f32[512,512]{0,1:T(8,128)} %copy.14, bf16[512,512]{1,0:T(8,128)(2,1)S(1)} %convolution_convert_fusion.3, bf16[6,512,512]{2,1,0:T(8,128)(2,1)} %all-gather.2.cloned.1.call-done), kind=kOutput, calls=%fused_computation.7 | convolution fusion | flops 268697600 | bytes 3145728 | tf_op jit(solution)/shard_map/dot_general | solution.py:26
  154.0 2.4 %convolution_convert_fusion.2 = bf16[512,512]{0,1:T(8,128)(2,1)S(1)} fusion(bf16[512,512]{1,0:T(8,128)(2,1)} %bitcast.105, f32[512,512]{0,1:T(8,128)} %copy.12, bf16[512,512]{1,0:T(8,128)(2,1)S(1)} %convolution_convert_fusion.3, bf16[6,512,512]{2,1,0:T(8,128)(2,1)} %all-gather.2.cloned.1.call-done), kind=kOutput, calls=%fused_computation.16 | convolution fusion | flops 537657344 | bytes 3145728 | tf_op jit(solution)/shard_map/dot_general | solution.py:31
  156.4 2.5 %fusion.1 = f32[512,512]{0,1:T(8,128)} fusion(f32[512,512]{0,1:T(8,128)S(1)} %fusion.2, bf16[512,512]{0,1:T(8,128)(2,1)S(1)} %convolution_convert_fusion.2, bf16[6,512,512]{2,1,0:T(8,128)(2,1)} %all-gather.2.cloned.1.call-done), kind=kOutput, calls=%fused_computation.5 | convolution fusion | flops 268697600 | bytes 3145728 | tf_op jit(solution)/shard_map/dot_general | solution.py:26
  158.9 2.9 %convolution_convert_fusion.1 = bf16[512,512]{0,1:T(8,128)(2,1)} fusion(bf16[512,512]{1,0:T(8,128)(2,1)} %bitcast.104, f32[512,512]{0,1:T(8,128)S(1)} %copy-done.2, bf16[512,512]{0,1:T(8,128)(2,1)S(1)} %convolution_convert_fusion.2, bf16[6,512,512]{2,1,0:T(8,128)(2,1)} %all-gather.2.cloned.1.call-done), kind=kOutput, calls=%fused_computation.15 | convolution fusion | flops 537657344 | bytes 3145728 | tf_op jit(solution)/shard_map/dot_general | solution.py:31
  161.9 2.3 %fusion.9 = bf16[512,512]{1,0:T(8,128)(2,1)S(1)} fusion(bf16[512,512]{1,0:T(8,128)(2,1)} %bitcast.103, f32[512,512]{0,1:T(8,128)S(1)} %copy-done.3, bf16[512,512]{0,1:T(8,128)(2,1)} %convolution_convert_fusion.1, bf16[6,512,512]{2,1,0:T(8,128)(2,1)} %all-gather.2.cloned.1.call-done), kind=kOutput, calls=%fused_computation.21 | convolution fusion | flops 537657344 | bytes 3145728 | tf_op jit(solution)/shard_map/dot_general | solution.py:31
  164.1 1.5 pad_maximum_fusion
  (12 shorter events, 0.1 us)
Async XLA Ops:
  9.7 64.7 %copy-start.5 = (bf16[4,16,512]{2,1,0:T(8,128)(2,1)S(1)}, bf16[4,16,512]{2,1,0:T(8,128)(2,1)}, u32[]{:S(2)}) copy-start(bf16[4,16,512]{2,1,0:T(8,128)(2,1)} %param.4) | copy-start | bytes 196612
  9.7 64.7 %all-to-all-start.1 = ((bf16[64,32,512]{2,0,1:T(8,128)(2,1)}), bf16[64,32,512]{2,0,1:T(8,128)(2,1)S(1)}, u32[]{:S(2)}, u32[]{:S(2)}) async-start(bf16[64,32,512]{2,0,1:T(8,128)(2,1)} %bitcast.98), calls=%async_computation.1 | async-start | bytes 4194304 | tf_op jit(solution)/shard_map/all_to_all | solution.py:20
  19.8 129.7 %all-gather.2.cloned.1.call-start = ((), (), s32[]{:S(2)}) async-start(), calls=%async_computation.2 | async-start | bytes 3244032 | tf_op jit(solution)/shard_map/all_gather | solution.py:12
  74.4 2.0 %copy-start = (bf16[64,32,512]{2,0,1:T(8,128)(2,1)}, bf16[64,32,512]{2,0,1:T(8,128)(2,1)S(1)}, u32[]{:S(2)}) copy-start(bf16[64,32,512]{2,0,1:T(8,128)(2,1)S(1)} %all-to-all-done.1) | copy-start | bytes 6291460
  76.4 71.4 %all-to-all-start = ((bf16[32,4,16,512]{3,2,1,0:T(8,128)(2,1)}), bf16[32,4,16,512]{3,2,1,0:T(8,128)(2,1)S(1)}, u32[]{:S(2)}, u32[]{:S(2)}) async-start(bf16[32,4,16,512]{3,2,1,0:T(8,128)(2,1)} %stack.2), calls=%async_computation | async-start | bytes 4194304 | tf_op jit(solution)/shard_map/all_to_all | solution.py:10
  147.8 1.3 copy-start.1
  153.9 5.0 %copy-start.2 = (f32[512,512]{0,1:T(8,128)S(1)}, f32[512,512]{0,1:T(8,128)}, u32[]{:S(2)}) copy-start(f32[512,512]{0,1:T(8,128)} %fusion.4) | copy-start | bytes 3145732
  158.9 2.9 %copy-start.3 = (f32[512,512]{0,1:T(8,128)S(1)}, f32[512,512]{0,1:T(8,128)}, u32[]{:S(2)}) copy-start(f32[512,512]{0,1:T(8,128)} %fusion.1) | copy-start | bytes 3145732
  161.9 2.3 %copy-start.4 = (bf16[512,512]{0,1:T(8,128)(2,1)S(1)}, bf16[512,512]{0,1:T(8,128)(2,1)}, u32[]{:S(2)}) copy-start(bf16[512,512]{0,1:T(8,128)(2,1)} %convolution_convert_fusion.1) | copy-start | bytes 1572868
Sparse Core Ops, SparseCore 0:
  23.8 120.5 all-gather.1

commit v2 on v0

--- a/solution.py
+++ b/solution.py
@@ -15,7 +15,10 @@
     groups = lax.axis_size("aux")
     rows = integrals.shape[1] // groups
     sectioned = integrals.reshape(width, groups, rows)
-    block = lax.all_to_all(sectioned, "aux", split_axis=1, concat_axis=0, tiled=True)
+    block = jnp.concatenate(
+        lax.all_to_all(jnp.stack(jnp.split(sectioned, lax.axis_size("aux"), axis=1)), "aux", 0, 0),
+        axis=0,
+    )
     columns = block.reshape(block.shape[0], block.shape[2])
     outs = []
     for k in range(count):

time: 210 us -> 211 us (level)
  local copies, waits for them, and re-layouts: 5.24 us -> 11.5 us
  waiting for transfers between devices: 110 us -> 104 us
    all_gather x1, waiting for transfers between devices: 24 us -> 17.1 us  [local(): lax.all_gather(inverses, 'aux', axis=1, tiled=True)]
    split x0 -> x2, local copies, waits for them, and re-layouts: none -> 4.54 us  [local(): jnp.split(sectioned, lax.axis_size('aux'), axis=1)]
    unnamed x2 -> x36, local copies, waits for them, and re-layouts: 0.01 us -> 2.77 us
  transfers between devices with their start and end apart: 2 -> 2, of which waited for: 2 -> 2; matrix products, arithmetic and copies ran while one was open for 4% -> 7% of each run, Pallas kernels for 0% -> 0%
where the time goes in v2:
time: 211 us; the launch traced here: 210 us
  waiting for transfers between devices  104 us (49%)
  blocking collectives  63.3 us (30%)
  matrix products  14.8 us (7%)
  between operations  13.8 us (7%)
  local copies, waits for them, and re-layouts  11.5 us (5%)
  other arithmetic  2.94 us (1%)
    all_gather x1, waiting for transfers between devices, local(): lax.all_gather(lower_blocks, 'aux', axis=1, tiled=True)  85.1 us
    all_to_all x1, blocking collectives, local(): lax.all_to_all(jnp.stack(jnp.split(sectioned, lax.axis_size('aux'), axis=...  63.3 us
    all_gather x1, waiting for transfers between devices, local(): lax.all_gather(inverses, 'aux', axis=1, tiled=True)  17.1 us
    dot_general x4, matrix products, local(): jnp.dot(inv_all[k], rest, preferred_element_type=jnp.float32)  9.29 us
    dot_general x3, matrix products, local(): jnp.dot(low_all[k * (k - 1) // 2 + j], outs[j], preferred_element_type=jn...  5.55 us
    split x2, local copies, waits for them, and re-layouts, local(): jnp.split(sectioned, lax.axis_size('aux'), axis=1)  4.54 us
  transfers between devices with their start and end apart: 2, of which 2 were waited for; matrix products, arithmetic and copies ran while one was open for 7% of the time, Pallas kernels for 0%

profile of v2, /device:TPU:64, one launch (start us, length us, event | category | flops | bytes accessed | tf_op | source)
XLA Modules:
  0.0 210.0 jit_solution(5672783405979722442)
XLA Ops:
  6.5 0.0 all-gather.3.cloned.1.call-start
  6.5 0.7 all-gather.3.cloned.1.call-update
  7.3 0.0 all-gather.5.cloned.1.call-start
  7.3 0.7 all-gather.5.cloned.1.call-update
  8.0 2.4 %copy.621 = bf16[8,8,32,512]{3,2,1,0:T(8,128)(2,1)S(1)} copy(bf16[8,8,32,512]{3,1,2,0:T(8,128)(2,1)} %bitcast.162) | data formatting | bytes 4194304
  10.4 1.7 fusion.12
  12.1 2.8 %fusion.11 = (bf16[64,1,512]{2,1,0:T(2,128)(2,1)S(1)}, bf16[64,1,512]{2,1,0:T(2,128)(2,1)S(1)}, bf16[64,1,512]{2,1,0:T(2,128)(2,1)S(1)}, bf16[64,1,512]{2,1,0:T(...) fusion(bf16[64,32,512]{2,1,0:T(8,128)(2,1)S(1)} %bitcast.160), kind=kLoop, calls=%fused_computation.67 | loop fusion | bytes 2490368 | tf_op jit(solution)/shard_map/split | solution.py:19
  15.6 63.3 %all_to_all.5 = bf16[32,64,1,512]{3,1,2,0:T(8,128)(2,1)S(1)} all-to-all(bf16[32,64,1,512]{3,1,2,0:T(8,128)(2,1)S(1)} %constant_dynamic-update-slice_fusion), channel_id=1, replica_groups=mesh['grp'=16,'aux'=32] {'aux'}, dimensions={0} | all-to-all | bytes 4194304 | tf_op jit(solution)/shard_map/all_to_all | solution.py:19
  78.9 1.0 fusion.10
  79.9 1.3 bitcast_convert_fusion
  81.2 0.3 copy.587
  81.5 0.2 bitcast_convert_fusion.2
  81.7 1.3 copy.586
  83.1 1.6 copy.588
  84.6 17.1 %all-gather.3.cloned.1.call-done = bf16[4,512,512]{2,1,0:T(8,128)(2,1)} async-done(((bf16[4,16,512]{2,1,0:T(8,128)(2,1)}), bf16[4,512,512]{2,1,0:T(8,128)(2,1)}) %all-gather.3.cloned.1.call-update) | async-done | bytes 2097168 | tf_op jit(solution)/shard_map/all_gather | solution.py:9
  101.7 1.5 convolution_convert_fusion
  103.2 85.1 %all-gather.5.cloned.1.call-done = bf16[6,512,512]{2,1,0:T(8,128)(2,1)} async-done(((bf16[6,16,512]{2,1,0:T(8,128)(2,1)}), bf16[6,512,512]{2,1,0:T(8,128)(2,1)}) %all-gather.5.cloned.1.call-update) | async-done | bytes 3145744 | tf_op jit(solution)/shard_map/all_gather | solution.py:10
  188.3 2.5 %fusion.4 = f32[512,512]{0,1:T(8,128)} fusion(f32[512,512]{0,1:T(8,128)S(1)} %copy.587, bf16[512,512]{0,1:T(8,128)(2,1)S(1)} %convolution_convert_fusion, bf16[6,512,512]{2,1,0:T(8,128)(2,1)} %all-gather.5.cloned.1.call-done), kind=kOutput, calls=%fused_computation.10 | convolution fusion | flops 268697600 | bytes 3145728 | tf_op jit(solution)/shard_map/dot_general | solution.py:27
  190.8 2.4 %convolution_convert_fusion.3 = bf16[512,512]{0,1:T(8,128)(2,1)S(1)} fusion(f32[512,512]{0,1:T(8,128)} %copy.586, bf16[512,512]{0,1:T(8,128)(2,1)S(1)} %convolution_convert_fusion, bf16[4,512,512]{2,1,0:T(8,128)(2,1)} %all-gather.3.cloned.1.call-done, bf16[6,512,512]{2,1,0:T(8,128)(2,1)} %all-gather.5.cloned.1.call-done), kind=kOutput, calls=%fused_computation.16 | convolution fusion | flops 537657344 | bytes 3145728 | tf_op jit(solution)/shard_map/dot_general | solution.py:32
  193.2 1.5 fusion.2
  194.7 3.2 %convolution_convert_fusion.2 = bf16[512,512]{0,1:T(8,128)(2,1)} fusion(f32[512,512]{0,1:T(8,128)} %fusion.4, bf16[512,512]{0,1:T(8,128)(2,1)S(1)} %convolution_convert_fusion.3, bf16[4,512,512]{2,1,0:T(8,128)(2,1)} %all-gather.3.cloned.1.call-done, bf16[6,512,512]{2,1,0:T(8,128)(2,1)} %all-gather.5.cloned.1.call-done), kind=kOutput, calls=%fused_computation.15 | convolution fusion | flops 537657344 | bytes 3145728 | tf_op jit(solution)/shard_map/dot_general | solution.py:32
  197.9 1.5 fusion.1
  199.5 2.3 %fusion.9 = bf16[512,512]{1,0:T(8,128)(2,1)S(1)} fusion(f32[512,512]{0,1:T(8,128)S(1)} %fusion.1, bf16[512,512]{0,1:T(8,128)(2,1)} %convolution_convert_fusion.2, bf16[4,512,512]{2,1,0:T(8,128)(2,1)} %all-gather.3.cloned.1.call-done, bf16[6,512,512]{2,1,0:T(8,128)(2,1)} %all-gather.5.cloned.1.call-done), kind=kOutput, calls=%fused_computation.20 | convolution fusion | flops 537657344 | bytes 3145728 | tf_op jit(solution)/shard_map/dot_general | solution.py:32
  201.7 1.5 pad_maximum_fusion
  (36 shorter events, 0.4 us)
Async XLA Ops:
  6.5 95.2 %all-gather.3.cloned.1.call-start = ((), (), s32[]{:S(2)}) async-start(), calls=%async_computation.1 | async-start | bytes 2162688 | tf_op jit(solution)/shard_map/all_gather | solution.py:9
  7.3 181.1 %all-gather.5.cloned.1.call-start = ((), (), s32[]{:S(2)}) async-start(), calls=%async_computation.2 | async-start | bytes 3244032 | tf_op jit(solution)/shard_map/all_gather | solution.py:10
  81.7 20.0 %copy-start = (bf16[8,64,1,512]{3,1,2,0:T(8,128)(2,1)S(1)}, bf16[8,64,1,512]{3,1,2,0:T(8,128)(2,1)}, u32[]{:S(2)}) copy-start(bf16[8,64,1,512]{3,1,2,0:T(8,128)(2,1)} %get-tuple-element.8) | copy-start | bytes 1572868
  199.4 2.3 %copy-start.1 = (bf16[512,512]{0,1:T(8,128)(2,1)S(1)}, bf16[512,512]{0,1:T(8,128)(2,1)}, u32[]{:S(2)}) copy-start(bf16[512,512]{0,1:T(8,128)(2,1)} %convolution_convert_fusion.2) | copy-start | bytes 1572868
Sparse Core Ops, SparseCore 0:
  10.5 91.1 all-gather.2
  104.9 83.3 all-gather.4
